TPU v7x, 256 devices: a whole 4x4x8 slice. The times are simulated.
256 devices in a mesh: rows: 32 (over y_lo, z, core), mz: 8 (over x, y_hi).
Axes of the slice: x: 4, y: 4 (y_hi: 2, y_lo: 2; y = y_hi * 2 + y_lo), z: 8, core: 2. Of those that a mesh axis runs over, the one named last changes fastest.
Arguments:
- raw_scans: float32 [12288, 49152], P('rows', 'mz'), may hold values from 0.02 to 4
- scan_shift: int32 [12288], P('rows'), may hold values from -16 to 15, as said below
- scan_weight: int32 [12288], P('rows'), may hold values from 0 to 255
- spectra_init: float32 [64, 49152], P(None, 'mz'), may hold values from 0.05 to 1
Outputs:
- concentrations: float32 [12288, 64], P('rows')
- spectra: float32 [64, 49152], P(None, 'mz')
Inputs may be any that keep to these rules, and one draw needn't show every extreme that they name: `scan_shift`: every aligned scan reads two raw scans of its own run; the first run holds 3088 scans, the last 3056, the others 12288 // 4; the offsets follow piecewise linear warps over segments of 32 rows counted from each run's start.
All inputs are finite; a program needn't handle non-finite values.
Results may differ from a plain program's by a relative error of at most 0.0003.
Values sent between devices are 32-bit elements; how exact they have to be, the bound alone decides.
A program may use at most 128 MiB of HBM per device.

v0:
```python
import jax
import jax.numpy as jnp
from jax import lax
from jax.sharding import PartitionSpec as P

MZ = 49152
HALO = 16
SWEEPS = 2


fraction_unit = 256.0
rms_epsilon = 1e-06
ridge_share = 0.01


def padded_2(block, sides, width):
    for axis, dim in sides:
        count = lax.axis_size(axis)
        forward = [(i, i + 1) for i in range(count - 1)]
        backward = [(target, source) for source, target in forward]
        low = lax.ppermute(
            lax.slice_in_dim(block, block.shape[dim] - width, None, axis=dim), axis, forward
        )
        high = lax.ppermute(lax.slice_in_dim(block, 0, width, axis=dim), axis, backward)
        block = jnp.concatenate([low, block, high], axis=dim)
    return block


def dot_highest(left, right):
    return jnp.dot(left, right, precision=lax.Precision.HIGHEST, preferred_element_type=jnp.float32)


def inner_rows(left, right):
    return lax.dot_general(
        left,
        right,
        (((0,), (0,)), ((), ())),
        precision=lax.Precision.HIGHEST,
        preferred_element_type=jnp.float32,
    )


def ridge_solve(gram, target):
    width_count = gram.shape[0]
    ridge_level = ridge_share * jnp.trace(gram) / width_count
    factor = jnp.linalg.cholesky(gram + ridge_level * jnp.eye(width_count, dtype=jnp.float32))
    return jax.scipy.linalg.cho_solve((factor, True), target)


def body(raw_scans, scan_shift, scan_weight, spectra_init):
    rows_here = raw_scans.shape[0]
    padded = padded_2(raw_scans, (("rows", 0),), HALO)
    row_index = jnp.arange(rows_here, dtype=jnp.int32) + scan_shift + HALO
    fraction = scan_weight.astype(jnp.float32) / fraction_unit
    lower_rows = jnp.take(padded, row_index, axis=0)
    upper_rows = jnp.take(padded, row_index + 1, axis=0)
    warped = lower_rows * (1.0 - fraction)[:, None] + upper_rows * fraction[:, None]
    spectra = spectra_init
    spectra_gram = lax.psum(dot_highest(spectra, spectra.T), "mz")
    concentrations = jnp.zeros((rows_here, spectra.shape[0]), jnp.float32)
    for sweep_index in range(SWEEPS):
        scores = lax.psum(dot_highest(warped, spectra.T), "mz")
        concentrations = jnp.maximum(ridge_solve(spectra_gram, scores.T).T, 0.0)
        local_gram = inner_rows(concentrations, concentrations)
        cross, concentration_gram = lax.psum(
            (inner_rows(concentrations, warped), local_gram), "rows"
        )
        raw_spectra = jnp.maximum(ridge_solve(concentration_gram, cross), 0.0)
        squares = lax.psum(jnp.sum(raw_spectra * raw_spectra, axis=1), "mz")
        scales = jnp.sqrt(squares / MZ + rms_epsilon)
        spectra = raw_spectra / scales[:, None]
        if sweep_index + 1 < SWEEPS:
            spectra_gram = lax.psum(dot_highest(spectra, spectra.T), "mz")
    return (concentrations, spectra)


def solution(mesh):
    return jax.shard_map(
        body,
        mesh=mesh,
        in_specs=(P("rows", "mz"), P("rows"), P("rows"), P(None, "mz")),
        out_specs=(P("rows", None), P(None, "mz")),
        check_vma=False,
    )
```

profile of v0, /device:TPU:1, one launch (start us, length us, event | category | flops | bytes accessed | tf_op | source)
XLA Modules:
  0.0 845.6 jit_solution(11479368638794638572)
XLA Ops:
  8.5 4.9 collective-permute-start
  16.8 34.9 %psum.70 = f32[64,64]{0,1:T(8,128)S(1)} all-reduce(f32[64,64]{0,1:T(8,128)S(1)} %fusion.28), channel_id=1, replica_groups=mesh['rows'=32,'mz'=8] {'mz'}, use_global_device_ids=true, to_apply=%region_0.1 | all-reduce | flops 4096 | bytes 32768 | tf_op jit(solution)/shard_map/psum | solution.py:59
  53.1 5.8 cholesky.74
  60.4 8.4 constant_dynamic-update-slice_fusion.1
  69.6 15.5 %gather_fusion.1 = f32[384,6144]{1,0:T(8,128)} fusion(f32[416,6144]{1,0:T(8,128)} %constant_dynamic-update-slice_fusion, s32[1024]{0:T(1024)S(1)} %get-tuple-element.18), kind=kCustom, calls=%fused_computation.1.clone | custom fusion | bytes 18875904 | tf_op jit(solution)/shard_map/jit(_take)/gather | solution.py:56
  85.1 16.0 %gather_fusion = f32[384,6144]{1,0:T(8,128)} fusion(f32[416,6144]{1,0:T(8,128)} %constant_dynamic-update-slice_fusion, s32[1024]{0:T(1024)S(1)} %get-tuple-element.19), kind=kCustom, calls=%fused_computation.clone | custom fusion | bytes 18875904 | tf_op jit(solution)/shard_map/jit(_take)/gather | solution.py:55
  101.1 8.2 fusion
  112.9 8.1 convolution_bitcast_fusion
  121.8 4.9 custom-call.14
  126.7 84.1 %all-reduce.5.cloned.1.call-done = f32[64,384]{0,1:T(8,128)} async-done(((f32[64,384]{0,1:T(8,128)}), f32[64,384]{0,1:T(8,128)}) %all-reduce.5.cloned.1.call-update) | async-done | bytes 98320 | tf_op jit(solution)/shard_map/psum | solution.py:62
  212.4 12.3 %fusion.30 = f32[64,6144]{1,0:T(8,128)} fusion(f32[64,384]{1,0:T(8,128)S(1)} %convolution_maximum_fusion.3, f32[384,6144]{1,0:T(8,128)} %copy-done.1), kind=kOutput, calls=%fused_computation.82 | convolution fusion | flops 1811939328 | bytes 11108352 | tf_op jit(solution)/shard_map/dot_general | solution.py:34
  225.0 105.9 %psum.72 = f32[64,64]{0,1:T(8,128)S(1)} all-reduce(f32[64,64]{0,1:T(8,128)S(1)} %fusion.29), channel_id=1, replica_groups=mesh['rows'=32,'mz'=8] {'rows'}, use_global_device_ids=true, to_apply=%region_5.9 | all-reduce | flops 4096 | bytes 32768 | tf_op jit(solution)/shard_map/psum | solution.py:65
  332.3 5.8 cholesky.85
  344.4 110.1 %all-reduce.7.cloned.1.call-done = f32[64,6144]{1,0:T(8,128)} async-done(((f32[64,6144]{1,0:T(8,128)}), f32[64,6144]{1,0:T(8,128)}) %all-reduce.7.cloned.1.call-update) | async-done | bytes 1572880 | tf_op jit(solution)/shard_map/psum | solution.py:65
  459.0 20.3 %psum.74 = f32[64]{0:T(128)S(1)} all-reduce(f32[64]{0:T(128)S(1)} %get-tuple-element.14), channel_id=1, replica_groups=mesh['rows'=32,'mz'=8] {'mz'}, use_global_device_ids=true, to_apply=%region_9.14 | all-reduce | flops 64 | bytes 512 | tf_op jit(solution)/shard_map/psum | solution.py:69
  479.3 12.2 %fusion.1 = f32[64,384]{1,0:T(8,128)} fusion(f32[384,6144]{1,0:T(8,128)} %copy-done.1, f32[64,6144]{1,0:T(8,128)S(1)} %get-tuple-element.15, f32[64]{0:T(128)S(1)} %add_sqrt_fusion.1), kind=kOutput, calls=%fused_computation.14 | convolution fusion | flops 1812332544 | bytes 11108608 | tf_op jit(solution)/shard_map/dot_general | solution.py:30
  493.2 30.0 %psum.75 = f32[64,64]{0,1:T(8,128)S(1)} all-reduce(f32[64,64]{0,1:T(8,128)S(1)} %fusion.2), channel_id=1, replica_groups=mesh['rows'=32,'mz'=8] {'mz'}, use_global_device_ids=true, to_apply=%region_10.15 | all-reduce | flops 4096 | bytes 32768 | tf_op jit(solution)/shard_map/psum | solution.py:73
  524.6 5.8 cholesky.96
  536.7 33.7 %all-reduce.9.cloned.1.call-done = f32[64,384]{1,0:T(8,128)} async-done(((f32[64,384]{1,0:T(8,128)}), f32[64,384]{1,0:T(8,128)}) %all-reduce.9.cloned.1.call-update) | async-done | bytes 98320 | tf_op jit(solution)/shard_map/psum | solution.py:62
  571.8 12.1 %fusion.32 = f32[64,6144]{1,0:T(8,128)} fusion(f32[64,384]{1,0:T(8,128)S(1)} %convolution_maximum_fusion.2, f32[384,6144]{1,0:T(8,128)} %copy-done.1), kind=kOutput, calls=%fused_computation.84 | convolution fusion | flops 1811939328 | bytes 11108352 | tf_op jit(solution)/shard_map/dot_general | solution.py:34
  584.2 106.2 %psum.77 = f32[64,64]{0,1:T(8,128)S(1)} all-reduce(f32[64,64]{0,1:T(8,128)S(1)} %fusion.31), channel_id=1, replica_groups=mesh['rows'=32,'mz'=8] {'rows'}, use_global_device_ids=true, to_apply=%region_13.18 | all-reduce | flops 4096 | bytes 32768 | tf_op jit(solution)/shard_map/psum | solution.py:65
  691.8 5.8 cholesky.107
  703.8 108.9 %all-reduce.11.cloned.1.call-done = f32[64,6144]{1,0:T(8,128)} async-done(((f32[64,6144]{1,0:T(8,128)}), f32[64,6144]{1,0:T(8,128)}) %all-reduce.11.cloned.1.call-update) | async-done | bytes 1572880 | tf_op jit(solution)/shard_map/psum | solution.py:65
  817.2 20.0 %psum.79 = f32[64]{0:T(128)S(1)} all-reduce(f32[64]{0:T(128)S(1)} %get-tuple-element.16), channel_id=1, replica_groups=mesh['rows'=32,'mz'=8] {'mz'}, use_global_device_ids=true, to_apply=%region_17.22 | all-reduce | flops 64 | bytes 512 | tf_op jit(solution)/shard_map/psum | solution.py:69
  (74 shorter events, 48.2 us)
Async XLA Ops:
  7.2 8.3 copy-start
  7.2 8.2 copy-start.3
  7.2 203.6 %all-reduce.5.cloned.1.call-start = ((), (), s32[]{:S(2)}) async-start(), calls=%async_computation | async-start | bytes 393216 | tf_op jit(solution)/shard_map/psum | solution.py:62
  8.5 51.1 %collective-permute-start = (f32[16,6144]{1,0:T(8,128)S(1)}, f32[16,6144]{1,0:T(8,128)S(1)}, u32[]{:S(2)}, u32[]{:S(2)}) collective-permute-start(f32[16,6144]{1,0:T(8,128)S(1)} %get-tuple-element.6), channel_id=1, source_target_pairs={{0,8},{8,16},{16,24},{24,32},{32,40},{40,48},{48,56},{56,64},{64,7... | collective-permute-start | bytes 1179656 | tf_op jit(solution)/shard_map/ppermute | solution.py:21
  13.5 55.4 %collective-permute-start.1 = (f32[16,6144]{1,0:T(8,128)S(1)}, f32[16,6144]{1,0:T(8,128)S(1)}, u32[]{:S(2)}, u32[]{:S(2)}) collective-permute-start(f32[16,6144]{1,0:T(8,128)S(1)} %get-tuple-element.4), channel_id=1, source_target_pairs={{8,0},{16,8},{24,16},{32,24},{40,32},{48,40},{56,48},{64,56},{72,6... | collective-permute-start | bytes 1179656 | tf_op jit(solution)/shard_map/ppermute | solution.py:24
  15.4 44.2 %copy-start.4 = (s32[384]{0:T(512)S(1)}, s32[384]{0:T(512)}, u32[]{:S(2)}) copy-start(s32[384]{0:T(512)} %param.13) | copy-start | bytes 4612
  109.3 3.6 copy-start.1
  121.1 333.5 %all-reduce.7.cloned.1.call-start = ((), (), s32[]{:S(2)}) async-start(), calls=%async_computation.1 | async-start | bytes 3145728 | tf_op jit(solution)/shard_map/psum | solution.py:65
  224.7 345.7 %all-reduce.9.cloned.1.call-start = ((), (), s32[]{:S(2)}) async-start(), calls=%async_computation.2 | async-start | bytes 196608 | tf_op jit(solution)/shard_map/psum | solution.py:62
  493.2 319.6 %all-reduce.11.cloned.1.call-start = ((), (), s32[]{:S(2)}) async-start(), calls=%async_computation.3 | async-start | bytes 3145728 | tf_op jit(solution)/shard_map/psum | solution.py:65
  571.8 12.1 %copy-start.2 = (f32[64,384]{1,0:T(8,128)}, f32[64,384]{1,0:T(8,128)S(1)}, u32[]{:S(2)}) copy-start(f32[64,384]{1,0:T(8,128)S(1)} %convolution_maximum_fusion.2) | copy-start | bytes 294916
Sparse Core Ops, SparseCore 0:
  121.2 89.5 all-reduce.4
  224.8 229.6 all-reduce.6
  493.3 77.0 all-reduce.8
  584.1 228.6 all-reduce.10
where the time goes:
time: 854 us; the launch traced here: 846 us
  waiting for transfers between devices  337 us (39%)
  blocking collectives  317 us (37%)
  other arithmetic  60.4 us (7%)
  matrix products  60.1 us (7%)
  local copies, waits for them, and re-layouts  46.6 us (5%)
  between operations  17.2 us (2%)
    psum x2, waiting for transfers between devices, body(): lax.psum((inner_rows(concentrations, warped), local_gram), 'rows')  219 us
    psum x2, blocking collectives, body(): lax.psum((inner_rows(concentrations, warped), local_gram), 'rows')  212 us
    psum x2, waiting for transfers between devices, body(): scores = lax.psum(dot_highest(warped, spectra.T), 'mz')  118 us
    psum x2, blocking collectives, body(): spectra_gram = lax.psum(dot_highest(spectra, spectra.T), 'mz')  64.9 us
    psum x2, blocking collectives, body(): squares = lax.psum(jnp.sum(raw_spectra * raw_spectra, axis=1), 'mz')  40.3 us
    another operation x12, other arithmetic, ridge_solve(): jnp.linalg.cholesky(gram + ridge_level * jnp.eye(width_count, dtype=jnp.f...  26.1 us
    dot_general x4, matrix products, inner_rows(): lax.dot_general(left, right, (((0,), (0,)), ((), ())), precision=lax.Prec...  24.9 us
    dot_general x4, matrix products, dot_highest(): jnp.dot(left, right, precision=lax.Precision.HIGHEST, preferred_element_t...  23.3 us
  transfers between devices with their start and end apart: 6, of which 4 were waited for; matrix products, arithmetic and copies ran while one was open for 7% of the time, Pallas kernels for 0%

commit v1 on v0

v1 whole, which is shorter than its diff:
```python
import functools

import jax
import jax.numpy as jnp
from jax import lax
from jax.experimental import pallas as pl
from jax.experimental.pallas import tpu as pltpu
from jax.sharding import PartitionSpec as P

MESH = pl.DeviceIdType.MESH
F32 = jnp.float32
BF16 = jnp.bfloat16

MZ = 49152
K = 64
HALO = 16
SWEEPS = 2
ROW_DEVS = 32
MZ_DEVS = 8
RING = 8
ROWS = 384
PADDED = ROWS + 2 * HALO
TALL = 512
COLS = 6144
BLOCK = COLS // RING
HALF = BLOCK // 2
TILE = 128

fraction_unit = 256.0
rms_epsilon = 1e-06
ridge_share = 0.01

ORDER = (4, 3, 5, 2, 6, 1, 7, 0)


def split(x):
    high = x.astype(BF16)
    return high, (x - high.astype(F32)).astype(BF16)


def dot(left, right, dims, precision=None):
    return lax.dot_general(
        left, right, (dims, ((), ())), precision=precision, preferred_element_type=F32
    )


NN = ((1,), (0,))
NT = ((1,), (1,))
TN = ((0,), (0,))
HIGHEST = lax.Precision.HIGHEST


def iota(shape, dim):
    return lax.broadcasted_iota(jnp.int32, shape, dim)


def pack_gram(gram):
    return jnp.concatenate([gram[: K // 2], gram[K // 2 :]], axis=1)


def unpack_gram(packed):
    return jnp.concatenate([packed[:, :K], packed[:, K:]], axis=0)


def factor_start(gram):
    eye = iota((K, K), 0) == iota((K, K), 1)
    diagonal = jnp.where(eye, gram, 0.0)
    trace = jnp.sum(jnp.sum(diagonal, axis=1, keepdims=True), axis=0, keepdims=True)
    ridge = ridge_share * trace / K
    unit = jnp.where(eye, 1.0, 0.0).astype(F32)
    joined = jnp.concatenate([gram + unit * ridge, unit], axis=1)
    return tuple(joined[8 * j : 8 * j + 8] for j in range(8))


def factor_steps(groups, first, last):
    sub = iota((8, 1), 0)

    def step(g, groups):
        groups = list(groups)
        for p in range(8):
            pivot = groups[0][p : p + 1, p : p + 1]
            inverse = lax.rsqrt(pivot)
            inverse = inverse * (1.5 - 0.5 * pivot * inverse * inverse)
            row = groups[0][p : p + 1, :] * inverse
            for j in range(1, 8):
                column = jnp.where(j < 8 - g, groups[j][:, p : p + 1] * inverse, 0.0)
                groups[j] = groups[j] - column * row
            column = jnp.where(sub > p, groups[0][:, p : p + 1] * inverse, 0.0)
            groups[0] = jnp.where(sub == p, row, groups[0] - column * row)
        rolled = [pltpu.roll(x, 2 * K - 8, 1) for x in groups]
        return tuple(rolled[1:] + rolled[:1])

    return lax.fori_loop(first, last, step, groups)


def factor_end(groups):
    return jnp.concatenate(groups, axis=0)[:, :K]


def solve(inverse_factor, target):
    return dot(inverse_factor, dot(inverse_factor, target, NN, HIGHEST), TN, HIGHEST)


def kernel(
    raw, shift, weight, spec, conc_out, spec_out,
    raw32, spec32, halo32, high, low, spec2, halo2, warp, acc, gram_acc,
    gram_send, gram_recv, score_send, score_recv, score_sum, score_all,
    conc_gram, conc_gram_core, conc_gram_pair, conc_gram_y, conc_gram_all,
    spread, spread2, cross, cross_core, chain_up, chain_down, cross_y,
    found, square_recv, load_sem, send_sem, recv_sem,
):
    ri = lax.axis_index("rows")
    mj = lax.axis_index("mz")
    core = lax.rem(ri, 2)
    z = lax.rem(lax.div(ri, 2), RING)
    plane = ri - 2 * z

    def at_z(distance):
        return lax.rem(z + distance, RING)

    def z_device(distance):
        return plane + 2 * at_z(distance)

    partner = ri + 1 - 2 * core
    y_pair = lax.rem(ri + 16, ROW_DEVS)
    row_next = lax.rem(ri + 1, ROW_DEVS)
    row_back = lax.rem(ri + ROW_DEVS - 1, ROW_DEVS)
    started = []

    def send(source, target, rows=None, mz=None):
        number = len(started)
        copy = pltpu.make_async_remote_copy(
            src_ref=source,
            dst_ref=target,
            send_sem=send_sem.at[number],
            recv_sem=recv_sem.at[number],
            device_id=(ri if rows is None else rows, mj if mz is None else mz),
            device_id_type=MESH,
        )
        copy.start()
        started.append(copy)
        return copy

    def block_columns(b):
        return pl.ds(pl.multiple_of(b * BLOCK, TILE), BLOCK)

    spec_load = pltpu.make_async_copy(spec, spec32, load_sem.at[RING])
    spec_load.start()
    loads = []
    for b in range(RING):
        columns = pl.ds(b * BLOCK, BLOCK)
        loads.append(pltpu.make_async_copy(raw.at[:, columns], raw32.at[:, columns], load_sem.at[b]))
        loads[-1].start()

    barrier = pltpu.get_barrier_semaphore()
    peers = [(ri, lax.rem(mj + d, MZ_DEVS)) for d in range(1, MZ_DEVS)]
    peers += [(z_device(d), mj) for d in range(1, RING)]
    peers += [(y_pair, mj), (row_next, mj), (row_back, mj)]
    for peer in peers:
        pl.semaphore_signal(barrier, inc=1, device_id=peer, device_id_type=MESH)

    for t in range(3):
        target = iota((2 * TILE, TILE), 1) + shift[:, t * TILE : (t + 1) * TILE] + HALO
        fraction = weight[:, t * TILE : (t + 1) * TILE].astype(F32) / fraction_unit
        row = iota((2 * TILE, TILE), 0)
        warp[t] = jnp.where(row == target, 1.0 - fraction, 0.0) + jnp.where(
            row == target + 1, fraction, 0.0
        )
    acc[...] = jnp.zeros_like(acc)
    gram_acc[...] = jnp.zeros_like(gram_acc)

    pl.semaphore_wait(barrier, len(peers))
    halo_up = send(raw.at[pl.ds(ROWS - HALO, HALO), :], halo32.at[0], rows=row_next)
    halo_down = send(raw.at[pl.ds(0, HALO), :], halo32.at[1], rows=row_back)

    def square(b):
        part = spec2[:, block_columns(b)]
        gram_acc[...] += dot(part, part, NT)

    def gram_of():
        total = gram_acc[...]
        total = total[:K] + total[K:]
        return total[:, :K] + total[:, K:]

    def send_gram(s):
        packed = pack_gram(gram_of())
        gram_send[s] = packed
        gram_recv[s, mj] = packed
        return [
            send(gram_send.at[s], gram_recv.at[s, mj], mz=lax.rem(mj + d, MZ_DEVS))
            for d in range(1, MZ_DEVS)
        ]

    def gram_sum(s, copies):
        for copy in copies:
            copy.wait_recv()
        total = gram_recv[s, 0]
        for j in range(1, MZ_DEVS):
            total = total + gram_recv[s, j]
        return unpack_gram(total)

    spec_load.wait()

    def first_spectra(b, carry):
        columns = block_columns(b)
        upper, lower = split(spec32[:, columns])
        spec2[:K, columns] = upper
        spec2[K:, columns] = lower
        square(b)
        return carry

    lax.fori_loop(0, RING, first_spectra, 0)
    gram_copies = send_gram(0)

    for b in range(RING):
        loads[b].wait()
        columns = pl.ds(b * BLOCK, BLOCK)

        def split_rows(r, carry):
            rows = pl.multiple_of(r * 32, 32)
            upper, lower = split(raw32[pl.ds(rows, 32), columns])
            rows = pl.multiple_of(rows + HALO, HALO)
            high[pl.ds(rows, 32), columns] = upper
            low[pl.ds(rows, 32), columns] = lower
            return carry

        lax.fori_loop(0, ROWS // 32, split_rows, 0)
        part = spec2[:, columns]
        own = pl.ds(HALO, ROWS)
        acc[own, :] += dot(high[own, columns], part, NT) + dot(low[own, columns], part, NT)

    halo_up.wait_recv()
    halo_down.wait_recv()

    def halo_block(b, carry):
        columns = block_columns(b)
        for side, rows in ((0, pl.ds(0, HALO)), (1, pl.ds(HALO + ROWS, HALO))):
            upper, lower = split(halo32[side, :, columns])
            high[rows, columns] = upper
            low[rows, columns] = lower
            halo2[side * HALO : (side + 1) * HALO, :] = upper
            halo2[(side + 2) * HALO : (side + 3) * HALO, :] = lower
        total = dot(halo2[...], spec2[:, columns], NT)
        total = total[: 2 * HALO] + total[2 * HALO :]
        acc[:HALO, :] += total[:HALO]
        acc[HALO + ROWS : PADDED, :] += total[HALO:]
        return carry

    lax.fori_loop(0, RING, halo_block, 0)

    for s in range(SWEEPS):
        for t in range(3):
            part = dot(acc[t * TILE : (t + 2) * TILE, :], warp[t], TN, HIGHEST)
            score_send[s, :, t * TILE : (t + 1) * TILE] = part[:K] + part[K:]
        copies = []
        for d in range(1, MZ_DEVS):
            j = lax.rem(mj + d, MZ_DEVS)
            rows = pl.ds(pl.multiple_of(j * 8, 8), 8)
            copies.append(send(score_send.at[s, rows], score_recv.at[s, d], mz=j))
        gram = gram_sum(s, gram_copies)
        if s > 0:
            eye = iota((K, K), 0) == iota((K, K), 1)
            diagonal = jnp.where(eye, gram, 0.0)
            down = 1.0 / jnp.sqrt(jnp.sum(diagonal, axis=1, keepdims=True) / MZ + rms_epsilon)
            across = 1.0 / jnp.sqrt(jnp.sum(diagonal, axis=0, keepdims=True) / MZ + rms_epsilon)
            gram = gram * down * across
        groups = factor_steps(factor_start(gram), 0, 4)
        own = pl.ds(pl.multiple_of(mj * 8, 8), 8)
        total = score_send[s, own]
        for d in range(1, MZ_DEVS):
            copies[d - 1].wait_recv()
            total = total + score_recv[s, d]
        score_sum[s] = total
        score_all[s, own] = total
        copies = [
            send(score_sum.at[s], score_all.at[s, own], mz=lax.rem(mj + d, MZ_DEVS))
            for d in range(1, MZ_DEVS)
        ]
        inverse = factor_end(factor_steps(groups, 4, 8))
        for copy in copies:
            copy.wait_recv()
        scores = score_all[s]
        if s > 0:
            scores = scores * down
        conc = jnp.maximum(solve(inverse, scores), 0.0)
        if s == SWEEPS - 1:
            conc_out[...] = conc.T

        packed = pack_gram(dot(conc, conc, NT, HIGHEST))
        conc_gram[s] = packed
        gram_copy = send(conc_gram.at[s], conc_gram_core.at[s], rows=partner)

        spread[...] = jnp.zeros_like(spread)
        for t in range(3):
            part = dot(conc[:, t * TILE : (t + 1) * TILE], warp[t], NT, HIGHEST)
            spread[:, t * TILE : (t + 2) * TILE] += part
        upper, lower = split(spread[...])
        spread2[:K] = upper
        spread2[K:] = lower

        core_copies = {}

        def cross_block(i):
            columns = block_columns(at_z(ORDER[i]))
            left = spread2[:, :PADDED]
            part = dot(left, high[:, columns], NN) + dot(left, low[:, columns], NN)
            part = part[:K] + part[K:]
            cross[s, i, 0] = part[:, :HALF]
            cross[s, i, 1] = part[:, HALF:]
            core_copies[i] = send(cross.at[s, i, 1 - core], cross_core.at[s, i], rows=partner)

        def cross_add(i):
            core_copies[i].wait_recv()
            cross[s, i, core] += cross_core[s, i]

        UPPER, LOWER, BOTH = pl.ds(0, K // 2), pl.ds(K // 2, K // 2), pl.ds(0, K)

        def chain_send(step, first, second):
            part = BOTH if step else UPPER
            one = send(cross.at[s, first, core, part], chain_up.at[s, step, part], rows=z_device(1))
            part = BOTH if step else LOWER
            two = send(cross.at[s, second, core, part], chain_down.at[s, step, part], rows=z_device(7))
            return one, two

        def chain_add(step, copies, first, second):
            copies[0].wait_recv()
            part = BOTH if step else UPPER
            cross[s, first, core, part] += chain_up[s, step, part]
            copies[1].wait_recv()
            part = BOTH if step else LOWER
            cross[s, second, core, part] += chain_down[s, step, part]

        cross_block(0)
        cross_block(1)
        cross_block(2)
        cross_add(0)
        chain = chain_send(0, 0, 0)
        gram_copy.wait_recv()
        packed = conc_gram[s] + conc_gram_core[s]
        conc_gram_pair[s] = packed
        gram_copy = send(conc_gram_pair.at[s], conc_gram_y.at[s], rows=y_pair)
        cross_block(3)
        cross_block(4)
        cross_add(1)
        cross_add(2)
        chain_add(0, chain, 1, 2)
        chain = chain_send(1, 1, 2)
        gram_copy.wait_recv()
        packed = conc_gram_pair[s] + conc_gram_y[s]
        conc_gram_all[s, z] = packed
        gram_copies = [
            send(conc_gram_all.at[s, z], conc_gram_all.at[s, z], rows=z_device(d))
            for d in range(1, RING)
        ]
        cross_block(5)
        cross_block(6)
        cross_add(3)
        cross_add(4)
        chain_add(1, chain, 3, 4)
        chain = chain_send(2, 3, 4)
        cross_block(7)
        cross_add(5)
        cross_add(6)
        for copy in gram_copies:
            copy.wait_recv()
        packed = conc_gram_all[s, 0]
        for d in range(1, RING):
            packed = packed + conc_gram_all[s, d]
        groups = factor_steps(factor_start(unpack_gram(packed)), 0, 2)
        chain_add(2, chain, 5, 6)
        chain = chain_send(3, 5, 6)
        cross_add(7)
        groups = factor_steps(groups, 2, 5)
        chain_add(3, chain, 7, 7)
        y_copy = send(cross.at[s, 7, core], cross_y.at[s], rows=y_pair)
        inverse = factor_end(factor_steps(groups, 5, 8))
        y_copy.wait_recv()
        block = cross[s, 7, core] + cross_y[s]
        found[s, core, z] = jnp.maximum(solve(inverse, block), 0.0)

        if s < SWEEPS - 1:
            acc[...] = jnp.zeros_like(acc)
        gram_acc[...] = jnp.zeros_like(gram_acc)

        def to_core(b):
            place = found.at[s, core, b]
            return send(place, place, rows=partner)

        def along(b, distance, part):
            place = found.at[s, core, b, part]
            return send(place, place, rows=z_device(distance))

        def use_block(b):
            columns = block_columns(b)
            if s < SWEEPS - 1:
                for c in range(2):
                    upper, lower = split(found[s, c, b])
                    spec2[:K, pl.ds(pl.multiple_of(b * BLOCK + c * HALF, TILE), HALF)] = upper
                    spec2[K:, pl.ds(pl.multiple_of(b * BLOCK + c * HALF, TILE), HALF)] = lower
                square(b)
                part = spec2[:, columns]
                acc[:PADDED, :] += dot(high[:, columns], part, NT) + dot(low[:, columns], part, NT)
            else:
                for c in range(2):
                    x = found[s, c, b]
                    x = x * x
                    gram_acc[:K, :] += (
                        x[:, :TILE] + x[:, TILE : 2 * TILE] + x[:, 2 * TILE :]
                    )

        up = along(z, 1, BOTH)
        down_way = along(z, 7, BOTH)
        ready = [(z, [to_core(z)])]
        for step in range(1, 5):
            up.wait_recv()
            below, above = at_z(RING - step), at_z(step)
            last = step == 4
            if not last:
                up = along(below, 1, BOTH if step < 3 else UPPER)
            down_way.wait_recv()
            if not last:
                down_way = along(above, 7, BOTH if step < 3 else LOWER)
            arrived = [(below, [to_core(below)])]
            if not last:
                arrived.append((above, [to_core(above)]))
            for b, copies in ready:
                for copy in copies:
                    copy.wait_recv()
                use_block(b)
            ready = arrived
        for b, copies in ready:
            for copy in copies:
                copy.wait_recv()
            use_block(b)
        if s < SWEEPS - 1:
            gram_copies = send_gram(s + 1)

    ones = jnp.ones((8, TILE), F32)
    squares = dot(ones, gram_acc[:K, :], NT, HIGHEST)
    square_recv[MZ_DEVS] = squares
    copies = [
        send(square_recv.at[MZ_DEVS], square_recv.at[mj], mz=lax.rem(mj + d, MZ_DEVS))
        for d in range(1, MZ_DEVS)
    ]
    square_recv[mj] = squares
    for copy in copies:
        copy.wait_recv()
    total = square_recv[0]
    for j in range(1, MZ_DEVS):
        total = total + square_recv[j]
    across = 1.0 / jnp.sqrt(total / MZ + rms_epsilon)
    down = across.T[:, :1]

    def write(b, carry):
        for c in range(2):
            spec_out[:, pl.ds(pl.multiple_of(b * BLOCK + c * HALF, TILE), HALF)] = (
                found[SWEEPS - 1, c, b] * down
            )
        return carry

    lax.fori_loop(0, RING, write, 0)
    for copy in started:
        copy.wait_send()


COPIES = 256


def body(raw_scans, scan_shift, scan_weight, spectra_init):
    any_space = pl.BlockSpec(memory_space=pl.ANY)
    vmem = pl.BlockSpec(memory_space=pltpu.VMEM)
    return pl.pallas_call(
        kernel,
        out_shape=(
            jax.ShapeDtypeStruct((ROWS, K), F32),
            jax.ShapeDtypeStruct((K, COLS), F32),
        ),
        in_specs=[any_space, vmem, vmem, any_space],
        out_specs=(vmem, vmem),
        scratch_shapes=[
            pltpu.VMEM((ROWS, COLS), F32),
            pltpu.VMEM((K, COLS), F32),
            pltpu.VMEM((2, HALO, COLS), F32),
            pltpu.VMEM((PADDED, COLS), BF16),
            pltpu.VMEM((PADDED, COLS), BF16),
            pltpu.VMEM((2 * K, COLS), BF16),
            pltpu.VMEM((4 * HALO, BLOCK), BF16),
            pltpu.VMEM((3, 2 * TILE, TILE), F32),
            pltpu.VMEM((TALL, 2 * K), F32),
            pltpu.VMEM((2 * K, 2 * K), F32),
            pltpu.VMEM((SWEEPS, K // 2, 2 * K), F32),
            pltpu.VMEM((SWEEPS, MZ_DEVS, K // 2, 2 * K), F32),
            pltpu.VMEM((SWEEPS, K, ROWS), F32),
            pltpu.VMEM((SWEEPS, MZ_DEVS, 8, ROWS), F32),
            pltpu.VMEM((SWEEPS, 8, ROWS), F32),
            pltpu.VMEM((SWEEPS, K, ROWS), F32),
            pltpu.VMEM((SWEEPS, K // 2, 2 * K), F32),
            pltpu.VMEM((SWEEPS, K // 2, 2 * K), F32),
            pltpu.VMEM((SWEEPS, K // 2, 2 * K), F32),
            pltpu.VMEM((SWEEPS, K // 2, 2 * K), F32),
            pltpu.VMEM((SWEEPS, RING, K // 2, 2 * K), F32),
            pltpu.VMEM((K, TALL), F32),
            pltpu.VMEM((2 * K, TALL), BF16),
            pltpu.VMEM((SWEEPS, RING, 2, K, HALF), F32),
            pltpu.VMEM((SWEEPS, RING, K, HALF), F32),
            pltpu.VMEM((SWEEPS, 4, K, HALF), F32),
            pltpu.VMEM((SWEEPS, 4, K, HALF), F32),
            pltpu.VMEM((SWEEPS, K, HALF), F32),
            pltpu.VMEM((SWEEPS, 2, RING, K, HALF), F32),
            pltpu.VMEM((MZ_DEVS + 1, 8, K), F32),
            pltpu.SemaphoreType.DMA((RING + 1,)),
            pltpu.SemaphoreType.DMA((COPIES,)),
            pltpu.SemaphoreType.DMA((COPIES,)),
        ],
        compiler_params=pltpu.CompilerParams(
            collective_id=0, has_side_effects=True, vmem_limit_bytes=56 * 1024 * 1024
        ),
        name="mcr_als",
    )(raw_scans, scan_shift.reshape(1, ROWS), scan_weight.reshape(1, ROWS), spectra_init)


def solution(mesh):
    return jax.shard_map(
        body,
        mesh=mesh,
        in_specs=(P("rows", "mz"), P("rows"), P("rows"), P(None, "mz")),
        out_specs=(P("rows", None), P(None, "mz")),
        check_vma=False,
    )
```

time: 854 us -> 150 us (0.18)
  waiting for transfers between devices: 337 us -> 0 us
  blocking collectives: 317 us -> 0 us
  Pallas kernels: 0 us -> 143 us
  other arithmetic: 60.4 us -> 0 us
  matrix products: 60.1 us -> 0 us
  local copies, waits for them, and re-layouts: 46.6 us -> 6.84 us
  between operations: 17.2 us -> 0.64 us
    psum x4 -> x0, waiting for transfers between devices: 337 us -> none  [the longest x2 219 us: body(): lax.psum((inner_rows(concentrations, warped), local_gram), 'rows')]
    psum x6 -> x0, blocking collectives: 317 us -> none  [the longest x2 212 us: body(): lax.psum((inner_rows(concentrations, warped), local_gram), 'rows')]
    pallas_call x0 -> x1, Pallas kernels: none -> 143 us  [body(): pl.pallas_call(kernel, out_shape=(jax.ShapeDtypeStruct((ROWS, K), F32), j...]
    another operation x20 -> x0, other arithmetic: 48.3 us -> none  [the longest x12 26.1 us: ridge_solve(): jnp.linalg.cholesky(gram + ridge_level * jnp.eye(width_count, dtype=jnp.f...]
    dot_general x8 -> x0, matrix products: 48.2 us -> none  [the longest x4 24.9 us: inner_rows(): lax.dot_general(left, right, (((0,), (0,)), ((), ())), precision=lax.Prec...]
    gather x2 -> x0, local copies, waits for them, and re-layouts: 31.4 us -> none  [the longest x1 16 us: body(): lower_rows = jnp.take(padded, row_index, axis=0)]
    another operation x8 -> x0, matrix products: 11.9 us -> none  [ridge_solve(): return jax.scipy.linalg.cho_solve((factor, True), target)]
    unnamed x12 -> x1, local copies, waits for them, and re-layouts: 12.8 us -> 2.66 us
  transfers between devices with their start and end apart: 6 -> 0, of which waited for: 4 -> 0; matrix products, arithmetic and copies ran while one was open for 7% -> 0% of each run, Pallas kernels for 0% -> 0%
where the time goes in v1:
time: 150 us
  Pallas kernels  143 us (95%)
  local copies, waits for them, and re-layouts  6.84 us (5%)
    pallas_call x1, Pallas kernels, body(): pl.pallas_call(kernel, out_shape=(jax.ShapeDtypeStruct((ROWS, K), F32), j...  143 us

profile of v1, /device:TPU:1, one launch (start us, length us, event | category | flops | bytes accessed | tf_op | source)
XLA Modules:
  0.0 150.0 jit_solution(6986332148169200296)
XLA Ops:
  0.6 1.2 reshape.10.shift
  1.9 1.2 reshape.11.weight
  3.1 142.6 %mcr_als.1 = (f32[384,64]{1,0:T(8,128)}, f32[64,6144]{1,0:T(8,128)}) custom-call(f32[384,6144]{1,0:T(8,128)} %raw.1, s32[1,384]{1,0:T(1,128)} %reshape.10.shift, s32[1,384]{1,0:T(1,128)} %reshape.11.weight, f32[64,6144]{1,0:T(8,128)} %spec.1), custom_call_target="tpu_custom_call" | custom-call | tf_op jit(solution)/shard_map/mcr_als/pallas_call | solution.py:472
  145.7 1.7 %copy.6 = f32[384,64]{0,1:T(8,128)} copy(f32[384,64]{1,0:T(8,128)} %get-tuple-element.2) | data formatting | bytes 196608 | tf_op jit(solution)/shard_map/mcr_als/pallas_call | solution.py:472
  147.4 2.7 %copy.8 = f32[64,6144]{1,0:T(8,128)} copy(f32[64,6144]{1,0:T(8,128)} %get-tuple-element.7) | data formatting | bytes 3145728

commit v2 on v1

v2 whole, which is shorter than its diff:
```python
import functools

import jax
import jax.numpy as jnp
from jax import lax
from jax.experimental import pallas as pl
from jax.experimental.pallas import tpu as pltpu
from jax.sharding import PartitionSpec as P

MESH = pl.DeviceIdType.MESH
F32 = jnp.float32
BF16 = jnp.bfloat16

MZ = 49152
K = 64
HALO = 16
SWEEPS = 2
ROW_DEVS = 32
MZ_DEVS = 8
RING = 8
ROWS = 384
PADDED = ROWS + 2 * HALO
TALL = 512
COLS = 6144
BLOCK = COLS // RING
HALF = BLOCK // 2
TILE = 128
HALO_PARTS = 2
LOADS = 4

fraction_unit = 256.0
rms_epsilon = 1e-06
ridge_share = 0.01

ORDER = (4, 3, 5, 2, 6, 1, 7, 0)
WAYS = ((1, 2), (7, 6))
HALVES = (pl.ds(0, K // 4), pl.ds(K // 4, K // 4))


def split(x):
    high = x.astype(BF16)
    return high, (x - high.astype(F32)).astype(BF16)


def dot(left, right, dims, precision=None):
    return lax.dot_general(
        left, right, (dims, ((), ())), precision=precision, preferred_element_type=F32
    )


NN = ((1,), (0,))
NT = ((1,), (1,))
TN = ((0,), (0,))
HIGHEST = lax.Precision.HIGHEST


def iota(shape, dim):
    return lax.broadcasted_iota(jnp.int32, shape, dim)


def pack_gram(gram):
    return jnp.concatenate([gram[: K // 2], gram[K // 2 :]], axis=1)


def unpack_gram(packed):
    return jnp.concatenate([packed[:, :K], packed[:, K:]], axis=0)


def factor_start(gram):
    eye = iota((K, K), 0) == iota((K, K), 1)
    diagonal = jnp.where(eye, gram, 0.0)
    trace = jnp.sum(jnp.sum(diagonal, axis=1, keepdims=True), axis=0, keepdims=True)
    ridge = ridge_share * trace / K
    unit = jnp.where(eye, 1.0, 0.0).astype(F32)
    joined = jnp.concatenate([gram + unit * ridge, unit], axis=1)
    return tuple(joined[8 * j : 8 * j + 8] for j in range(8))


def factor_steps(groups, first, last):
    sub = iota((8, 2 * K), 0)
    shape = (8, 2 * K)

    def step(g, groups):
        head = groups[0]
        columns = [jnp.broadcast_to(head[:, p : p + 1], shape) for p in range(8)]
        square = {}
        for p in range(8):
            for q in range(p, 8):
                square[q, p] = jnp.broadcast_to(columns[p][q : q + 1], shape)
        rows = [jnp.broadcast_to(head[p : p + 1], shape) for p in range(8)]
        inverse = []
        ratio = {}
        for p in range(8):
            inverse.append(1.0 / square[p, p])
            for q in range(p + 1, 8):
                ratio[q, p] = square[q, p] * inverse[p]
                for r in range(p + 1, q + 1):
                    square[q, r] = square[q, r] - ratio[q, p] * square[r, p]
                rows[q] = rows[q] - ratio[q, p] * rows[p]
        scaled = [rows[p] * inverse[p] for p in range(8)]
        done = rows[0]
        for p in range(8):
            root = lax.rsqrt(square[p, p])
            root = root * (1.5 - 0.5 * square[p, p] * root * root)
            done = jnp.where(sub == p, rows[p] * root, done)
        rest = []
        for j in range(1, 8):
            left = [groups[j][:, p : p + 1] for p in range(8)]
            left = [jnp.broadcast_to(x, shape) for x in left]
            for p in range(7):
                for q in range(p + 1, 8):
                    left[q] = left[q] - ratio[q, p] * left[p]
            terms = [left[p] * scaled[p] for p in range(8)]
            while len(terms) > 1:
                terms = [terms[i] + terms[i + 1] for i in range(0, len(terms), 2)]
            rest.append(groups[j] - jnp.where(j < 8 - g, terms[0], 0.0))
        return tuple(pltpu.roll(x, 2 * K - 8, 1) for x in rest + [done])

    return lax.fori_loop(first, last, step, groups)


def factor_end(groups):
    return jnp.concatenate(groups, axis=0)[:, :K]


def solve(inverse_factor, target):
    return dot(inverse_factor, dot(inverse_factor, target, NN, HIGHEST), TN, HIGHEST)


def kernel(
    raw, shift, weight, spec, conc_out, spec_out, scale_out,
    raw32, spec32, halo32, high, low, spec2, halo2, warp, acc,
    gram_send, gram_recv, score_send, score_recv, score_sum, score_all,
    conc_gram, conc_gram_core, conc_gram_pair, conc_gram_y, conc_gram_all, conc_gram_sum, conc_gram_total,
    spread, spread2, cross, cross_core, cross_y, far, farther, near, next_to, summed, owned,
    found, square_send, square_mz, square_z, square_y, load_sem, store_sem, send_sem, recv_sem,
):
    ri = lax.axis_index("rows")
    mj = lax.axis_index("mz")
    core = lax.rem(ri, 2)
    z = lax.rem(lax.div(ri, 2), RING)
    plane = ri - 2 * z

    def at_z(distance):
        return lax.rem(z + distance, RING)

    def z_device(distance):
        return plane + 2 * at_z(distance)

    def other_plane(device):
        return lax.rem(device + 16, ROW_DEVS)

    partner = ri + 1 - 2 * core
    y = lax.div(ri, 16)
    y_pair = lax.rem(ri + 16, ROW_DEVS)
    row_next = lax.rem(ri + 1, ROW_DEVS)
    row_back = lax.rem(ri + ROW_DEVS - 1, ROW_DEVS)
    started = []
    settled = []
    stores = []

    def send(source, target, rows=None, mz=None):
        number = len(started)
        copy = pltpu.make_async_remote_copy(
            src_ref=source,
            dst_ref=target,
            send_sem=send_sem.at[number],
            recv_sem=recv_sem.at[number],
            device_id=(ri if rows is None else rows, mj if mz is None else mz),
            device_id_type=MESH,
        )
        copy.start()
        started.append(copy)
        return copy

    def settle(keep):
        while len(settled) < len(started) - keep:
            started[len(settled)].wait_send()
            settled.append(True)

    def to_mz(source, target):
        return [
            send(source, target, mz=lax.rem(mj + d, MZ_DEVS)) for d in range(1, MZ_DEVS)
        ]

    def to_z(source, target):
        return [send(source, target, rows=z_device(d)) for d in range(1, RING)]

    def sum_slots(slots, count, copies):
        for copy in copies:
            copy.wait_recv()
        total = slots[0]
        for j in range(1, count):
            total = total + slots[j]
        return total

    def block_columns(b):
        return pl.ds(pl.multiple_of(b * BLOCK, TILE), BLOCK)

    spec_load = pltpu.make_async_copy(spec, spec32, load_sem.at[LOADS])
    spec_load.start()
    loads = []
    for b in range(LOADS):
        columns = pl.ds(b * (COLS // LOADS), COLS // LOADS)
        loads.append(pltpu.make_async_copy(raw.at[:, columns], raw32.at[:, columns], load_sem.at[b]))
        loads[-1].start()

    barrier = pltpu.get_barrier_semaphore()
    peers = [(ri, lax.rem(mj + d, MZ_DEVS)) for d in range(1, MZ_DEVS)]
    peers += [(z_device(d), mj) for d in range(1, RING)]
    peers += [(other_plane(z_device(d)), mj) for d in (1, 2, 6, 7)]
    peers += [(y_pair, mj), (row_next, mj), (row_back, mj)]
    for peer in peers:
        pl.semaphore_signal(barrier, inc=1, device_id=peer, device_id_type=MESH)

    pl.semaphore_wait(barrier, len(peers))
    halos = []
    for part in range(HALO_PARTS):
        columns = pl.ds(part * (COLS // HALO_PARTS), COLS // HALO_PARTS)
        halos.append((
            send(raw.at[pl.ds(ROWS - HALO, HALO), columns], halo32.at[0, :, columns], rows=row_next),
            send(raw.at[pl.ds(0, HALO), columns], halo32.at[1, :, columns], rows=row_back),
        ))

    for t in range(3):
        tile = pl.ds(t * TILE, TILE)
        target = iota((2 * TILE, TILE), 1) + shift[tile].reshape(1, TILE) + HALO
        fraction = weight[tile].reshape(1, TILE).astype(F32) / fraction_unit
        row = iota((2 * TILE, TILE), 0)
        warp[t] = jnp.where(row == target, 1.0 - fraction, 0.0) + jnp.where(
            row == target + 1, fraction, 0.0
        )
    acc[...] = jnp.zeros_like(acc)

    def send_gram(s):
        total = dot(spec2[...], spec2[...], NT)
        total = total[:K] + total[K:]
        packed = pack_gram(total[:, :K] + total[:, K:])
        gram_send[s] = packed
        gram_recv[s, mj] = packed
        return to_mz(gram_send.at[s], gram_recv.at[s, mj])

    spec_load.wait()

    def first_spectra(b, carry):
        columns = block_columns(b)
        upper, lower = split(spec32[:, columns])
        spec2[:K, columns] = upper
        spec2[K:, columns] = lower
        return carry

    lax.fori_loop(0, RING, first_spectra, 0)

    gram_copies = send_gram(0)

    for b in range(LOADS):
        loads[b].wait()
        columns = pl.ds(b * (COLS // LOADS), COLS // LOADS)

        def split_rows(r, carry):
            rows = pl.multiple_of(r * HALO, HALO)
            upper, lower = split(raw32[pl.ds(rows, HALO), columns])
            rows = pl.multiple_of(rows + HALO, HALO)
            high[pl.ds(rows, HALO), columns] = upper
            low[pl.ds(rows, HALO), columns] = lower
            return carry

        lax.fori_loop(0, ROWS // 16, split_rows, 0)
        part = spec2[:, columns]
        own = pl.ds(HALO, ROWS)
        acc[own, :] += dot(high[own, columns], part, NT) + dot(low[own, columns], part, NT)

    for part in range(HALO_PARTS):
        for copy in halos[part]:
            copy.wait_recv()
        columns = pl.ds(part * (COLS // HALO_PARTS), COLS // HALO_PARTS)
        for side, rows in ((0, pl.ds(0, HALO)), (1, pl.ds(HALO + ROWS, HALO))):
            upper, lower = split(halo32[side, :, columns])
            high[rows, columns] = upper
            low[rows, columns] = lower
            halo2[side * HALO : (side + 1) * HALO, :] = upper
            halo2[(side + 2) * HALO : (side + 3) * HALO, :] = lower
        total = dot(halo2[...], spec2[:, columns], NT)
        total = total[: 2 * HALO] + total[2 * HALO :]
        acc[:HALO, :] += total[:HALO]
        acc[HALO + ROWS : PADDED, :] += total[HALO:]

    for s in range(SWEEPS):
        last_sweep = s == SWEEPS - 1
        for t in range(3):
            part = dot(acc[t * TILE : (t + 2) * TILE, :], warp[t], TN, HIGHEST)
            score_send[s, :, t * TILE : (t + 1) * TILE] = part[:K] + part[K:]
        copies = []
        for d in range(1, MZ_DEVS):
            j = lax.rem(mj + d, MZ_DEVS)
            rows = pl.ds(pl.multiple_of(j * 8, 8), 8)
            copies.append(send(score_send.at[s, rows], score_recv.at[s, d], mz=j))
        if s > 0:
            gram_copies = send_gram(s)
        if s == 0:
            gram = unpack_gram(sum_slots(gram_recv.at[s], MZ_DEVS, gram_copies))
            inverse = factor_end(factor_steps(factor_start(gram), 0, 8))
        own = pl.ds(pl.multiple_of(mj * 8, 8), 8)
        total = score_send[s, own]
        for d in range(1, MZ_DEVS):
            copies[d - 1].wait_recv()
            total = total + score_recv[s, d]
        score_sum[s] = total
        score_all[s, own] = total
        copies = to_mz(score_sum.at[s], score_all.at[s, own])
        if s > 0:
            gram = unpack_gram(sum_slots(gram_recv.at[s], MZ_DEVS, gram_copies))
            eye = iota((K, K), 0) == iota((K, K), 1)
            diagonal = jnp.where(eye, gram, 0.0)
            down = 1.0 / jnp.sqrt(jnp.sum(diagonal, axis=1, keepdims=True) / MZ + rms_epsilon)
            across = 1.0 / jnp.sqrt(jnp.sum(diagonal, axis=0, keepdims=True) / MZ + rms_epsilon)
            gram = gram * down * across
            inverse = factor_end(factor_steps(factor_start(gram), 0, 8))
        settle(14)
        for copy in copies:
            copy.wait_recv()
        scores = score_all[s]
        if s > 0:
            scores = scores * down
        conc = jnp.maximum(solve(inverse, scores), 0.0)
        if last_sweep:
            conc_out[...] = conc

        spread[...] = jnp.zeros_like(spread)
        for t in range(3):
            part = dot(conc[:, t * TILE : (t + 1) * TILE], warp[t], NT, HIGHEST)
            spread[:, t * TILE : (t + 2) * TILE] += part
        upper, lower = split(spread[...])
        spread2[:K] = upper
        spread2[K:] = lower

        packed = pack_gram(dot(conc, conc, NT, HIGHEST))
        conc_gram[s] = packed
        gram_copy = send(conc_gram.at[s], conc_gram_core.at[s], rows=partner)

        core_copies = {}
        y_copies = {}

        def cross_blocks(*several):
            for i in several:
                columns = block_columns(at_z(ORDER[i]))
                left = spread2[:, :PADDED]
                part = dot(left, high[:, columns], NN) + dot(left, low[:, columns], NN)
                part = part[:K] + part[K:]
                for c in range(2):
                    for h in range(2):
                        cross[s, i, c, h] = part[c * 32 : c * 32 + 32, h * HALF : h * HALF + HALF]
            for i in several:
                core_copies[i] = send(
                    cross.at[s, i, 1 - core], cross_core.at[s, i], rows=partner
                )

        def cross_add(i):
            core_copies[i].wait_recv()
            cross[s, i, core] += cross_core[s, i]

        def to_y(i):
            y_copies[i] = send(cross.at[s, i, core, 1 - y], cross_y.at[s, i], rows=y_pair)

        def y_sum(i):
            y_copies[i].wait_recv()
            return cross[s, i, core, y] + cross_y[s, i]

        cross_blocks(0)
        cross_blocks(1, 2)
        cross_add(0)
        farther_copies = []
        for way in range(2):
            device = z_device(WAYS[way][1])
            farther_copies += [
                send(cross.at[s, 0, core, y, HALVES[way]], farther.at[s, way, 0], rows=device),
                send(
                    cross.at[s, 0, core, 1 - y, HALVES[way]],
                    farther.at[s, way, 1],
                    rows=other_plane(device),
                ),
            ]
        gram_copy.wait_recv()
        packed = conc_gram[s] + conc_gram_core[s]
        conc_gram_pair[s] = packed
        gram_copy = send(conc_gram_pair.at[s], conc_gram_y.at[s], rows=y_pair)
        far_copies = []
        for way in range(2):
            cross_add(1 + way)
            device = z_device(WAYS[way][0])
            far_copies += [
                send(cross.at[s, 1 + way, core, y], far.at[s, way, 0], rows=device),
                send(
                    cross.at[s, 1 + way, core, 1 - y], far.at[s, way, 1], rows=other_plane(device)
                ),
            ]
        cross_blocks(3, 4)
        cross_blocks(5, 6)
        for i in (3, 4):
            cross_add(i)
            to_y(i)
        gram_copy.wait_recv()
        packed = conc_gram_pair[s] + conc_gram_y[s]
        conc_gram_total[...] = packed
        part = conc_gram_total[pl.ds(pl.multiple_of(16 * core, 16), 16)]
        conc_gram_all[s, z] = part
        gram_copies = to_z(conc_gram_all.at[s, z], conc_gram_all.at[s, z])
        cross_blocks(7)
        for i in (5, 6, 7):
            cross_add(i)
            to_y(i)
        near_copies = []
        for way in range(2):
            total = y_sum(3 + way)
            for plane_copy in range(2):
                far_copies[2 * way + plane_copy].wait_recv()
                total = total + far[s, way, plane_copy]
            summed[s, 3 + way] = total
            for plane_copy in range(2):
                farther_copies[2 * way + plane_copy].wait_recv()
                summed[s, 3 + way, HALVES[way]] += farther[s, way, plane_copy]
            near_copies.append(
                send(summed.at[s, 3 + way], near.at[s, way], rows=z_device(WAYS[way][1]))
            )
        conc_gram_sum[s, core] = sum_slots(conc_gram_all.at[s], RING, gram_copies)
        gram_copy = send(conc_gram_sum.at[s, core], conc_gram_sum.at[s, core], rows=partner)
        next_copies = []
        for way in range(2):
            summed[s, 5 + way] = y_sum(5 + way)
            next_copies.append(
                send(summed.at[s, 5 + way], next_to.at[s, way], rows=z_device(WAYS[way][0]))
            )
        gram_copy.wait_recv()
        groups = factor_steps(
            factor_start(unpack_gram(conc_gram_sum[s].reshape(K // 2, 2 * K))), 0, 6
        )
        total = y_sum(7)
        for way in range(2):
            near_copies[way].wait_recv()
            total = total + near[s, way]
        for way in range(2):
            next_copies[way].wait_recv()
            total = total + next_to[s, way]
        owned[s, core] = total
        owned_copy = send(owned.at[s, core], owned.at[s, core], rows=partner)
        inverse = factor_end(factor_steps(groups, 6, 8))
        settle(16)
        owned_copy.wait_recv()
        block = jnp.maximum(solve(inverse, owned[s].reshape(K, HALF)), 0.0)
        found[s, :, z, y] = block.reshape(2, K // 2, HALF)

        def pass_on(b, device, rows=None, planes=None):
            place = found.at[s, core, b, y if planes is None else planes]
            if rows is not None:
                place = place.at[rows]
            return send(place, place, rows=device)

        def to_core(b):
            place = found.at[s, core, b]
            return send(place, place, rows=partner)

        def use_blocks(*several):
            for b in several:
                for c in range(2):
                    for h in range(2):
                        first = pl.multiple_of(b * BLOCK + h * HALF, TILE)
                        columns = pl.ds(first, HALF)
                        rows = pl.ds(c * 32, 32)
                        if last_sweep:
                            store = pltpu.make_async_copy(
                                found.at[s, c, b, h],
                                spec_out.at[rows, columns],
                                store_sem.at[len(stores)],
                            )
                            store.start()
                            stores.append(store)
                        else:
                            upper, lower = split(found[s, c, b, h])
                            spec2[rows, columns] = upper
                            spec2[pl.ds(K + c * 32, 32), columns] = lower
            if not last_sweep:
                total = acc[:PADDED, :]
                for b in several:
                    columns = block_columns(b)
                    part = spec2[:, columns]
                    total = total + dot(high[:, columns], part, NT)
                    total = total + dot(low[:, columns], part, NT)
                acc[:PADDED, :] = total

        one_away = [pass_on(z, z_device(WAYS[way][0])) for way in range(2)]
        two_away = [pass_on(z, z_device(WAYS[way][1])) for way in range(2)]
        over_y = [pass_on(z, y_pair)]
        if last_sweep:
            x = block * block
            x = x[:, :TILE] + x[:, TILE : 2 * TILE] + x[:, 2 * TILE :]
            squares = dot(jnp.ones((8, TILE), F32), x, NT, HIGHEST)
            square_send[0] = squares
            square_mz[mj] = squares
            square_copies = to_mz(square_send.at[0], square_mz.at[mj])
        else:
            acc[...] = jnp.zeros_like(acc)
        ones = [at_z(RING - 1), at_z(1)]
        twos = [at_z(RING - 2), at_z(2)]
        threes = [at_z(RING - 3), at_z(3)]
        four = at_z(4)
        for way in range(2):
            one_away[way].wait_recv()
            over_y.append(pass_on(ones[way], y_pair))
        three_away, four_away = [], []
        for way in range(2):
            two_away[way].wait_recv()
            device = z_device(WAYS[way][0])
            three_away.append(pass_on(twos[way], device))
            three_away.append(pass_on(twos[way], other_plane(device)))
            device = z_device(WAYS[way][1])
            four_away.append(pass_on(twos[way], device, HALVES[way]))
            four_away.append(pass_on(twos[way], other_plane(device), HALVES[way]))
            over_y.append(pass_on(twos[way], y_pair))
        over_y[0].wait_recv()
        over_core = [pass_on(z, partner, planes=1 - y)]
        if last_sweep:
            squares = sum_slots(square_mz, MZ_DEVS, square_copies)
            square_z[z] = squares
            square_copies = to_z(square_z.at[z], square_z.at[z])
        for way in range(2):
            over_y[1 + way].wait_recv()
            over_core.append(to_core(ones[way]))
        over_core[0].wait_recv()
        use_blocks(z)
        for way in range(2):
            over_y[3 + way].wait_recv()
            over_core.append(to_core(twos[way]))
        for way in range(2):
            over_core[1 + way].wait_recv()
        use_blocks(*ones)
        for way in range(2):
            three_away[2 * way].wait_recv()
            three_away[2 * way + 1].wait_recv()
            over_core.append(to_core(threes[way]))
        if last_sweep:
            squares = sum_slots(square_z, RING, square_copies)
            square_send[1] = squares
            square_copy = send(square_send.at[1], square_y, rows=y_pair)
        for copy in four_away:
            copy.wait_recv()
        over_core.append(to_core(four))
        for way in range(2):
            over_core[3 + way].wait_recv()
        use_blocks(*twos)
        for way in range(2):
            over_core[5 + way].wait_recv()
        over_core[7].wait_recv()
        use_blocks(*threes, four)
        if last_sweep:
            settle(12)

    square_copy.wait_recv()
    across = 1.0 / jnp.sqrt((squares + square_y[...]) / MZ + rms_epsilon)
    scale_out[...] = across[0]
    for store in stores:
        store.wait()
    settle(0)


COPIES = 200


def body(raw_scans, scan_shift, scan_weight, spectra_init):
    any_space = pl.BlockSpec(memory_space=pl.ANY)
    vmem = pl.BlockSpec(memory_space=pltpu.VMEM)
    conc, spectra, scale = pl.pallas_call(
        kernel,
        out_shape=(
            jax.ShapeDtypeStruct((K, ROWS), F32),
            jax.ShapeDtypeStruct((K, COLS), F32),
            jax.ShapeDtypeStruct((K,), F32),
        ),
        in_specs=[any_space, vmem, vmem, any_space],
        out_specs=(vmem, any_space, vmem),
        scratch_shapes=[
            pltpu.VMEM((ROWS, COLS), F32),
            pltpu.VMEM((K, COLS), F32),
            pltpu.VMEM((2, HALO, COLS), F32),
            pltpu.VMEM((PADDED, COLS), BF16),
            pltpu.VMEM((PADDED, COLS), BF16),
            pltpu.VMEM((2 * K, COLS), BF16),
            pltpu.VMEM((4 * HALO, COLS // HALO_PARTS), BF16),
            pltpu.VMEM((3, 2 * TILE, TILE), F32),
            pltpu.VMEM((TALL, 2 * K), F32),
            pltpu.VMEM((SWEEPS, K // 2, 2 * K), F32),
            pltpu.VMEM((SWEEPS, MZ_DEVS, K // 2, 2 * K), F32),
            pltpu.VMEM((SWEEPS, K, ROWS), F32),
            pltpu.VMEM((SWEEPS, MZ_DEVS, 8, ROWS), F32),
            pltpu.VMEM((SWEEPS, 8, ROWS), F32),
            pltpu.VMEM((SWEEPS, K, ROWS), F32),
            pltpu.VMEM((SWEEPS, K // 2, 2 * K), F32),
            pltpu.VMEM((SWEEPS, K // 2, 2 * K), F32),
            pltpu.VMEM((SWEEPS, K // 2, 2 * K), F32),
            pltpu.VMEM((SWEEPS, K // 2, 2 * K), F32),
            pltpu.VMEM((SWEEPS, RING, K // 4, 2 * K), F32),
            pltpu.VMEM((SWEEPS, 2, K // 4, 2 * K), F32),
            pltpu.VMEM((K // 2, 2 * K), F32),
            pltpu.VMEM((K, TALL), F32),
            pltpu.VMEM((2 * K, TALL), BF16),
            pltpu.VMEM((SWEEPS, RING, 2, 2, K // 2, HALF), F32),
            pltpu.VMEM((SWEEPS, RING, 2, K // 2, HALF), F32),
            pltpu.VMEM((SWEEPS, RING, K // 2, HALF), F32),
            pltpu.VMEM((SWEEPS, 2, 2, K // 2, HALF), F32),
            pltpu.VMEM((SWEEPS, 2, 2, K // 4, HALF), F32),
            pltpu.VMEM((SWEEPS, 2, K // 2, HALF), F32),
            pltpu.VMEM((SWEEPS, 2, K // 2, HALF), F32),
            pltpu.VMEM((SWEEPS, RING, K // 2, HALF), F32),
            pltpu.VMEM((SWEEPS, 2, K // 2, HALF), F32),
            pltpu.VMEM((SWEEPS, 2, RING, 2, K // 2, HALF), F32),
            pltpu.VMEM((2, 8, K), F32),
            pltpu.VMEM((MZ_DEVS, 8, K), F32),
            pltpu.VMEM((RING, 8, K), F32),
            pltpu.VMEM((8, K), F32),
            pltpu.SemaphoreType.DMA((LOADS + 1,)),
            pltpu.SemaphoreType.DMA((4 * RING,)),
            pltpu.SemaphoreType.DMA((COPIES,)),
            pltpu.SemaphoreType.DMA((COPIES,)),
        ],
        compiler_params=pltpu.CompilerParams(
            collective_id=0, has_side_effects=True, vmem_limit_bytes=56 * 1024 * 1024
        ),
        name="mcr_als",
    )(raw_scans, scan_shift, scan_weight, spectra_init)
    return conc.T, spectra * scale[:, None]


def solution(mesh):
    return jax.shard_map(
        body,
        mesh=mesh,
        in_specs=(P("rows", "mz"), P("rows"), P("rows"), P(None, "mz")),
        out_specs=(P("rows", None), P(None, "mz")),
        check_vma=False,
    )
```

time: 150 us -> 125 us (0.83)
  Pallas kernels: 143 us -> 121 us
  local copies, waits for them, and re-layouts: 6.84 us -> 0.64 us
  other arithmetic: 0 us -> 2.77 us
    pallas_call x1, Pallas kernels: 143 us -> 121 us  [body(): pl.pallas_call(kernel, out_shape=(jax.ShapeDtypeStruct((K, ROWS), F32), j...]
    mul x0 -> x1, other arithmetic: none -> 2.77 us  [body(): return (conc.T, spectra * scale[:, None])]
    reshape x2 -> x0, local copies, waits for them, and re-layouts: 2.49 us -> none  [the longest x1 1.25 us: body(): scan_shift.reshape(1, ROWS)]
    unnamed x1 -> x3, local copies, waits for them, and re-layouts: 2.66 us -> 0.64 us
    pallas_call x1 -> x0, local copies, waits for them, and re-layouts: 1.68 us -> none  [body(): pl.pallas_call(kernel, out_shape=(jax.ShapeDtypeStruct((ROWS, K), F32), j...]
where the time goes in v2:
time: 125 us
  Pallas kernels  121 us (97%)
  other arithmetic  2.77 us (2%)
    pallas_call x1, Pallas kernels, body(): pl.pallas_call(kernel, out_shape=(jax.ShapeDtypeStruct((K, ROWS), F32), j...  121 us
    mul x1, other arithmetic, body(): return (conc.T, spectra * scale[:, None])  2.77 us

profile of v2, /device:TPU:1, one launch (start us, length us, event | category | flops | bytes accessed | tf_op | source)
XLA Modules:
  0.0 124.6 jit_solution(4775946930077979465)
XLA Ops:
  0.6 120.6 %mcr_als.1 = (f32[64,384]{1,0:T(8,128)}, f32[64,6144]{1,0:T(8,128)}, f32[64]{0:T(128)}) custom-call(f32[384,6144]{1,0:T(8,128)} %raw.1, s32[384]{0:T(512)} %shift.1, s32[384]{0:T(512)} %weight.1, f32[64,6144]{1,0:T(8,128)} %spec.1), custom_call_target="tpu_custom_call" | custom-call | tf_op jit(solution)/shard_map/mcr_als/pallas_call | solution.py:571
  121.2 0.0 copy-start
  121.2 2.8 %broadcast_multiply_fusion = f32[64,6144]{1,0:T(8,128)} fusion(f32[64,6144]{1,0:T(8,128)} %get-tuple-element.6, f32[64]{0:T(128)} %get-tuple-element.7), kind=kLoop, calls=%fused_computation | loop fusion | flops 393216 | bytes 3145984 | tf_op jit(solution)/shard_map/mul | solution.py:629
  124.0 0.0 copy-done
  124.0 0.6 copy.7
Async XLA Ops:
  121.2 2.8 %copy-start = (f32[64,384]{1,0:T(8,128)S(1)}, f32[64,384]{1,0:T(8,128)}, u32[]{:S(2)}) copy-start(f32[64,384]{1,0:T(8,128)} %get-tuple-element.5) | copy-start | bytes 294916

commit v3 on v2

--- a/solution.py
+++ b/solution.py
@@ -297,6 +297,7 @@
             copies.append(send(score_send.at[s, rows], score_recv.at[s, d], mz=j))
         if s > 0:
             gram_copies = send_gram(s)
+            settle(14)
         if s == 0:
             gram = unpack_gram(sum_slots(gram_recv.at[s], MZ_DEVS, gram_copies))
             inverse = factor_end(factor_steps(factor_start(gram), 0, 8))
@@ -316,7 +317,6 @@
             across = 1.0 / jnp.sqrt(jnp.sum(diagonal, axis=0, keepdims=True) / MZ + rms_epsilon)
             gram = gram * down * across
             inverse = factor_end(factor_steps(factor_start(gram), 0, 8))
-        settle(14)
         for copy in copies:
             copy.wait_recv()
         scores = score_all[s]
@@ -366,8 +366,11 @@
             y_copies[i].wait_recv()
             return cross[s, i, core, y] + cross_y[s, i]
 
-        cross_blocks(0)
-        cross_blocks(1, 2)
+        cross_blocks(0, 1, 2)
+        gram_copy.wait_recv()
+        packed = conc_gram[s] + conc_gram_core[s]
+        conc_gram_pair[s] = packed
+        gram_copy = send(conc_gram_pair.at[s], conc_gram_y.at[s], rows=y_pair)
         cross_add(0)
         farther_copies = []
         for way in range(2):
@@ -380,10 +383,6 @@
                     rows=other_plane(device),
                 ),
             ]
-        gram_copy.wait_recv()
-        packed = conc_gram[s] + conc_gram_core[s]
-        conc_gram_pair[s] = packed
-        gram_copy = send(conc_gram_pair.at[s], conc_gram_y.at[s], rows=y_pair)
         far_copies = []
         for way in range(2):
             cross_add(1 + way)
@@ -409,6 +408,7 @@
         for i in (5, 6, 7):
             cross_add(i)
             to_y(i)
+        settle(14)
         near_copies = []
         for way in range(2):
             total = y_sum(3 + way)
@@ -422,19 +422,19 @@
             near_copies.append(
                 send(summed.at[s, 3 + way], near.at[s, way], rows=z_device(WAYS[way][1]))
             )
-        conc_gram_sum[s, core] = sum_slots(conc_gram_all.at[s], RING, gram_copies)
-        gram_copy = send(conc_gram_sum.at[s, core], conc_gram_sum.at[s, core], rows=partner)
         next_copies = []
         for way in range(2):
             summed[s, 5 + way] = y_sum(5 + way)
             next_copies.append(
                 send(summed.at[s, 5 + way], next_to.at[s, way], rows=z_device(WAYS[way][0]))
             )
+        conc_gram_sum[s, core] = sum_slots(conc_gram_all.at[s], RING, gram_copies)
+        gram_copy = send(conc_gram_sum.at[s, core], conc_gram_sum.at[s, core], rows=partner)
+        total = y_sum(7)
         gram_copy.wait_recv()
         groups = factor_steps(
-            factor_start(unpack_gram(conc_gram_sum[s].reshape(K // 2, 2 * K))), 0, 6
+            factor_start(unpack_gram(conc_gram_sum[s].reshape(K // 2, 2 * K))), 0, 4
         )
-        total = y_sum(7)
         for way in range(2):
             near_copies[way].wait_recv()
             total = total + near[s, way]
@@ -443,8 +443,7 @@
             total = total + next_to[s, way]
         owned[s, core] = total
         owned_copy = send(owned.at[s, core], owned.at[s, core], rows=partner)
-        inverse = factor_end(factor_steps(groups, 6, 8))
-        settle(16)
+        inverse = factor_end(factor_steps(groups, 4, 8))
         owned_copy.wait_recv()
         block = jnp.maximum(solve(inverse, owned[s].reshape(K, HALF)), 0.0)
         found[s, :, z, y] = block.reshape(2, K // 2, HALF)
@@ -487,9 +486,9 @@
                     total = total + dot(low[:, columns], part, NT)
                 acc[:PADDED, :] = total
 
+        over_y = [pass_on(z, y_pair)]
         one_away = [pass_on(z, z_device(WAYS[way][0])) for way in range(2)]
         two_away = [pass_on(z, z_device(WAYS[way][1])) for way in range(2)]
-        over_y = [pass_on(z, y_pair)]
         if last_sweep:
             x = block * block
             x = x[:, :TILE] + x[:, TILE : 2 * TILE] + x[:, 2 * TILE :]
@@ -511,7 +510,6 @@
             two_away[way].wait_recv()
             device = z_device(WAYS[way][0])
             three_away.append(pass_on(twos[way], device))
-            three_away.append(pass_on(twos[way], other_plane(device)))
             device = z_device(WAYS[way][1])
             four_away.append(pass_on(twos[way], device, HALVES[way]))
             four_away.append(pass_on(twos[way], other_plane(device), HALVES[way]))
@@ -528,14 +526,16 @@
         over_core[0].wait_recv()
         use_blocks(z)
         for way in range(2):
+            three_away[way].wait_recv()
+            over_y.append(pass_on(threes[way], y_pair))
+        for way in range(2):
             over_y[3 + way].wait_recv()
             over_core.append(to_core(twos[way]))
         for way in range(2):
             over_core[1 + way].wait_recv()
         use_blocks(*ones)
         for way in range(2):
-            three_away[2 * way].wait_recv()
-            three_away[2 * way + 1].wait_recv()
+            over_y[5 + way].wait_recv()
             over_core.append(to_core(threes[way]))
         if last_sweep:
             squares = sum_slots(square_z, RING, square_copies)

time: 125 us -> 123 us (0.984)
  Pallas kernels: 121 us -> 119 us
    pallas_call x1, Pallas kernels: 121 us -> 119 us  [body(): pl.pallas_call(kernel, out_shape=(jax.ShapeDtypeStruct((K, ROWS), F32), j...]
where the time goes in v3:
time: 123 us
  Pallas kernels  119 us (97%)
  other arithmetic  2.77 us (2%)
    pallas_call x1, Pallas kernels, body(): pl.pallas_call(kernel, out_shape=(jax.ShapeDtypeStruct((K, ROWS), F32), j...  119 us
    mul x1, other arithmetic, body(): return (conc.T, spectra * scale[:, None])  2.77 us

profile of v3, /device:TPU:1, one launch (start us, length us, event | category | flops | bytes accessed | tf_op | source)
XLA Modules:
  0.0 123.2 jit_solution(9880084348365458060)
XLA Ops:
  0.6 119.1 %mcr_als.1 = (f32[64,384]{1,0:T(8,128)}, f32[64,6144]{1,0:T(8,128)}, f32[64]{0:T(128)}) custom-call(f32[384,6144]{1,0:T(8,128)} %raw.1, s32[384]{0:T(512)} %shift.1, s32[384]{0:T(512)} %weight.1, f32[64,6144]{1,0:T(8,128)} %spec.1), custom_call_target="tpu_custom_call" | custom-call | tf_op jit(solution)/shard_map/mcr_als/pallas_call | solution.py:571
  119.8 0.0 copy-start
  119.8 2.8 %broadcast_multiply_fusion = f32[64,6144]{1,0:T(8,128)} fusion(f32[64,6144]{1,0:T(8,128)} %get-tuple-element.6, f32[64]{0:T(128)} %get-tuple-element.7), kind=kLoop, calls=%fused_computation | loop fusion | flops 393216 | bytes 3145984 | tf_op jit(solution)/shard_map/mul | solution.py:629
  122.6 0.0 copy-done
  122.6 0.6 copy.7
Async XLA Ops:
  119.8 2.8 %copy-start = (f32[64,384]{1,0:T(8,128)S(1)}, f32[64,384]{1,0:T(8,128)}, u32[]{:S(2)}) copy-start(f32[64,384]{1,0:T(8,128)} %get-tuple-element.5) | copy-start | bytes 294916

commit v4 on v3

--- a/solution.py
+++ b/solution.py
@@ -383,16 +383,9 @@
                     rows=other_plane(device),
                 ),
             ]
-        far_copies = []
-        for way in range(2):
-            cross_add(1 + way)
-            device = z_device(WAYS[way][0])
-            far_copies += [
-                send(cross.at[s, 1 + way, core, y], far.at[s, way, 0], rows=device),
-                send(
-                    cross.at[s, 1 + way, core, 1 - y], far.at[s, way, 1], rows=other_plane(device)
-                ),
-            ]
+        for i in (1, 2):
+            cross_add(i)
+            to_y(i)
         cross_blocks(3, 4)
         cross_blocks(5, 6)
         for i in (3, 4):
@@ -404,6 +397,12 @@
         part = conc_gram_total[pl.ds(pl.multiple_of(16 * core, 16), 16)]
         conc_gram_all[s, z] = part
         gram_copies = to_z(conc_gram_all.at[s, z], conc_gram_all.at[s, z])
+        far_copies = []
+        for way in range(2):
+            summed[s, 1 + way] = y_sum(1 + way)
+            far_copies.append(
+                send(summed.at[s, 1 + way], far.at[s, way], rows=z_device(WAYS[way][0]))
+            )
         cross_blocks(7)
         for i in (5, 6, 7):
             cross_add(i)
@@ -412,9 +411,8 @@
         near_copies = []
         for way in range(2):
             total = y_sum(3 + way)
-            for plane_copy in range(2):
-                far_copies[2 * way + plane_copy].wait_recv()
-                total = total + far[s, way, plane_copy]
+            far_copies[way].wait_recv()
+            total = total + far[s, way]
             summed[s, 3 + way] = total
             for plane_copy in range(2):
                 farther_copies[2 * way + plane_copy].wait_recv()
@@ -605,7 +603,7 @@
             pltpu.VMEM((SWEEPS, RING, 2, 2, K // 2, HALF), F32),
             pltpu.VMEM((SWEEPS, RING, 2, K // 2, HALF), F32),
             pltpu.VMEM((SWEEPS, RING, K // 2, HALF), F32),
-            pltpu.VMEM((SWEEPS, 2, 2, K // 2, HALF), F32),
+            pltpu.VMEM((SWEEPS, 2, K // 2, HALF), F32),
             pltpu.VMEM((SWEEPS, 2, 2, K // 4, HALF), F32),
             pltpu.VMEM((SWEEPS, 2, K // 2, HALF), F32),
             pltpu.VMEM((SWEEPS, 2, K // 2, HALF), F32),

time: 123 us -> 121 us (0.984)
  Pallas kernels: 119 us -> 117 us
    pallas_call x1, Pallas kernels: 119 us -> 117 us  [body(): pl.pallas_call(kernel, out_shape=(jax.ShapeDtypeStruct((K, ROWS), F32), j...]
where the time goes in v4:
time: 121 us
  Pallas kernels  117 us (97%)
  other arithmetic  2.77 us (2%)
    pallas_call x1, Pallas kernels, body(): pl.pallas_call(kernel, out_shape=(jax.ShapeDtypeStruct((K, ROWS), F32), j...  117 us
    mul x1, other arithmetic, body(): return (conc.T, spectra * scale[:, None])  2.77 us

profile of v4, /device:TPU:1, one launch (start us, length us, event | category | flops | bytes accessed | tf_op | source)
XLA Modules:
  0.0 120.9 jit_solution(9807143840757904714)
XLA Ops:
  0.6 116.8 %mcr_als.1 = (f32[64,384]{1,0:T(8,128)}, f32[64,6144]{1,0:T(8,128)}, f32[64]{0:T(128)}) custom-call(f32[384,6144]{1,0:T(8,128)} %raw.1, s32[384]{0:T(512)} %shift.1, s32[384]{0:T(512)} %weight.1, f32[64,6144]{1,0:T(8,128)} %spec.1), custom_call_target="tpu_custom_call" | custom-call | tf_op jit(solution)/shard_map/mcr_als/pallas_call | solution.py:569
  117.5 0.0 copy-start
  117.5 2.8 %broadcast_multiply_fusion = f32[64,6144]{1,0:T(8,128)} fusion(f32[64,6144]{1,0:T(8,128)} %get-tuple-element.6, f32[64]{0:T(128)} %get-tuple-element.7), kind=kLoop, calls=%fused_computation | loop fusion | flops 393216 | bytes 3145984 | tf_op jit(solution)/shard_map/mul | solution.py:627
  120.3 0.0 copy-done
  120.3 0.6 copy.7
Async XLA Ops:
  117.5 2.8 %copy-start = (f32[64,384]{1,0:T(8,128)S(1)}, f32[64,384]{1,0:T(8,128)}, u32[]{:S(2)}) copy-start(f32[64,384]{1,0:T(8,128)} %get-tuple-element.5) | copy-start | bytes 294916
